TPU v7x, 128 devices: a whole 4x4x4 slice. The times are simulated.
128 devices in a mesh: fam: 4 (over z), ctx: 32 (over x, y, core).
Axes of the slice: x: 4, y: 4, z: 4, core: 2. Of those that a mesh axis runs over, the one named last changes fastest.
Arguments:
- queries: bfloat16 [4, 16384, 1024], P('fam', 'ctx'), may hold values from -7 to 7
- key_rows: bfloat16 [4, 16384, 1024], P('fam', 'ctx'), may hold values from -4 to 4
- value_rows: bfloat16 [4, 16384, 1024], P('fam', 'ctx'), may hold values from -6 to 6
- cotangent: bfloat16 [4, 16384, 1024], P('fam', 'ctx'), may hold values from -6 to 6
- out_weight: bfloat16 [1024, 1024], replicated, may hold values from -0.1875 to 0.1875
- prot_blocks: int32 [4, 32], P('fam'), may hold values from 1 to 8, 128 in all within a row
- last_fill: int32 [4, 32], P('fam'), may hold values from 1 to 128
- memory_slots: int32 [4, 512], P('fam'), may hold values from 0 to 511
Outputs:
- query_grad: bfloat16 [4, 16384, 1024], P('fam', 'ctx')
- key_grad: bfloat16 [4, 16384, 1024], P('fam', 'ctx')
- value_grad: bfloat16 [4, 16384, 1024], P('fam', 'ctx')
- weight_grad: float32 [1024, 1024], replicated
Inputs may be any that keep to these rules, and one draw needn't show every extreme that they name: `prot_blocks`: each family's protein lengths, in blocks, sum to 128, and the longest has exactly 8 blocks.
All inputs are finite; a program needn't handle non-finite values.
Results may differ from a plain program's by a relative error of at most 0.015.
Values may be sent and summed in bfloat16 or wider, within the bound.
A program may use at most 128 MiB of HBM per device.

v0:
```python
import jax
import jax.numpy as jnp
from jax import lax
from jax.sharding import PartitionSpec as P

HEAD_DIM = 64
W = 512
BLK = 128
NEG_FILL = -1e30


def passed_along(value, axis, steps):
    count = lax.axis_size(axis)
    initial, last = (max(0, -steps), min(count, count - steps))
    return lax.ppermute(value, axis, [(source, source + steps) for source in range(initial, last)])


def protein_tables(prot_blocks, last_fill):
    prot_ends = jnp.cumsum(prot_blocks)
    starts = prot_ends - prot_blocks
    valid_len = (prot_blocks - 1) * BLK + last_fill
    return (prot_ends, starts, valid_len)


def token_info(positions, tables):
    prot_ends, starts, valid_len = tables
    prot_count = prot_ends.shape[0]
    block_ids = jnp.floor_divide(positions, BLK)
    protein = jnp.sum((block_ids[:, None] >= prot_ends[None, :]).astype(jnp.int32), axis=1)
    onehot = protein[:, None] == jnp.arange(prot_count, dtype=jnp.int32)[None, :]
    first_block = jnp.sum(jnp.where(onehot, starts[None, :], 0), axis=1)
    allowed = jnp.sum(jnp.where(onehot, valid_len[None, :], 0), axis=1)
    is_valid = (positions >= 0) & (protein < prot_count) & (positions - first_block * BLK < allowed)
    return (protein, is_valid)


def band_mask(query_pos, query_info, key_pos, key_info):
    return (
        query_info[1][:, None]
        & key_info[1][None, :]
        & (query_info[0][:, None] == key_info[0][None, :])
        & (key_pos[None, :] <= query_pos[:, None])
        & (query_pos[:, None] - key_pos[None, :] < W)
    )


def columns_of(array, column, span):
    return lax.dynamic_slice_in_dim(array, column, span, 1)


def add_into(target, update, row_start, column):
    row_index = jnp.asarray(row_start, jnp.int32)
    current = lax.dynamic_slice(target, (row_index, column), update.shape)
    return lax.dynamic_update_slice(target, current + update, (row_index, column))


def attend(query_blk, grad_blk, key_blk, value_blk, live_mask):
    scale = HEAD_DIM ** (-0.5)
    scores = (
        jnp.einsum("qge,kge->gqk", query_blk, key_blk, preferred_element_type=jnp.float32) * scale
    )
    live = live_mask[None]
    shifted = jnp.where(live, scores, NEG_FILL)
    row_max = jnp.max(shifted, axis=-1, keepdims=True)
    expo = jnp.where(live, jnp.exp(shifted - row_max), 0.0)
    row_sum = jnp.maximum(jnp.sum(expo, axis=-1, keepdims=True), 1.0)
    attn_prob = expo / row_sum
    prob_half = attn_prob.astype(jnp.bfloat16)
    attended = jnp.einsum(
        "gqk,kge->qge", prob_half, value_blk, preferred_element_type=jnp.float32
    ).astype(jnp.bfloat16)
    grad_prob = jnp.einsum("qge,kge->gqk", grad_blk, value_blk, preferred_element_type=jnp.float32)
    row_dot = jnp.sum(attn_prob * grad_prob, axis=-1, keepdims=True)
    grad_score = (attn_prob * (grad_prob - row_dot) * scale).astype(jnp.bfloat16)
    grad_query = jnp.einsum("gqk,kge->qge", grad_score, key_blk, preferred_element_type=jnp.float32)
    grad_key = jnp.einsum("gqk,qge->kge", grad_score, query_blk, preferred_element_type=jnp.float32)
    grad_value = jnp.einsum("gqk,qge->kge", prob_half, grad_blk, preferred_element_type=jnp.float32)
    return (attended, grad_query, grad_key, grad_value, row_max, row_sum, row_dot)


def per_device(
    queries, key_rows, value_rows, cotangent, out_weight, prot_blocks, last_fill, memory_slots
):
    query_loc = queries[0]
    key_loc = key_rows[0]
    value_loc = value_rows[0]
    grad_out = cotangent[0]
    tables = protein_tables(prot_blocks[0], last_fill[0])
    slots = memory_slots[0]
    tokens, width = query_loc.shape
    span = 2 * HEAD_DIM
    pair_count = width // span
    heads_total = width // HEAD_DIM
    ctx_size = lax.axis_size("ctx")
    ctx_index = lax.axis_index("ctx")
    slot_total = slots.shape[0]
    slot_dev = slot_total // ctx_size
    base = ctx_index * tokens
    positions = base + jnp.arange(tokens, dtype=jnp.int32)
    own_info = token_info(positions, tables)
    ext_pos = base - W + jnp.arange(W + tokens, dtype=jnp.int32)
    ext_info = token_info(ext_pos, tables)
    source = jnp.arange(slot_total, dtype=jnp.int32) // slot_dev * tokens + slots
    mem_info = token_info(source, tables)
    own_slots = lax.dynamic_slice_in_dim(slots, ctx_index * slot_dev, slot_dev)
    mem_keys, mem_values = (
        lax.all_gather(key_loc[own_slots], "ctx", axis=0, tiled=True),
        lax.all_gather(value_loc[own_slots], "ctx", axis=0, tiled=True),
    )
    halo_keys, halo_values = passed_along((key_loc, value_loc), "ctx", 1)
    ext_keys = jnp.concatenate([halo_keys, key_loc], axis=0)
    ext_values = jnp.concatenate([halo_values, value_loc], axis=0)
    grad_attn = jnp.einsum(
        "te,de->td", grad_out, out_weight, preferred_element_type=jnp.float32
    ).astype(jnp.bfloat16)
    masks = []
    query_info = (own_info[0], own_info[1])
    key_info = (ext_info[0], ext_info[1])
    band = band_mask(positions, query_info, ext_pos, key_info)
    memory = (
        query_info[1][:, None]
        & mem_info[1][None, :]
        & (mem_info[0][None, :] < query_info[0][:, None])
    )
    masks.append(jnp.concatenate([band, memory], axis=1))

    def pair_step(head_pair, carry):
        (
            query_grad,
            band_kgrad,
            band_vgrad,
            mem_kgrad,
            mem_vgrad,
            attn_rows,
            stat_max,
            stat_sum,
            stat_dot,
        ) = carry
        column = head_pair * span
        query_pair = columns_of(query_loc, column, span).reshape(tokens, 2, HEAD_DIM)
        dout_pair = columns_of(grad_attn, column, span).reshape(tokens, 2, HEAD_DIM)
        key_band = columns_of(ext_keys, column, span).reshape(W + tokens, 2, HEAD_DIM)
        value_band = columns_of(ext_values, column, span).reshape(W + tokens, 2, HEAD_DIM)
        key_memory = columns_of(mem_keys, column, span).reshape(slot_total, 2, HEAD_DIM)
        value_memory = columns_of(mem_values, column, span).reshape(slot_total, 2, HEAD_DIM)
        key_blk = jnp.concatenate([key_band, key_memory], axis=0)
        value_blk = jnp.concatenate([value_band, value_memory], axis=0)
        attended, grad_query, grad_key, grad_value, row_max, row_sum, row_dot = attend(
            query_pair, dout_pair, key_blk, value_blk, masks[0]
        )
        row_index = jnp.asarray(0, jnp.int32)
        query_grad = lax.dynamic_update_slice(
            query_grad, grad_query.reshape(W, span), (row_index, column)
        )
        attn_rows = lax.dynamic_update_slice(
            attn_rows, attended.reshape(W, span), (row_index, column)
        )
        band_kgrad = add_into(band_kgrad, grad_key[: 2 * W].reshape(2 * W, span), 0, column)
        band_vgrad = add_into(band_vgrad, grad_value[: 2 * W].reshape(2 * W, span), 0, column)
        mem_kgrad = add_into(mem_kgrad, grad_key[2 * W :].reshape(slot_total, span), 0, column)
        mem_vgrad = add_into(mem_vgrad, grad_value[2 * W :].reshape(slot_total, span), 0, column)
        stat_col = head_pair * 2
        zero_row = jnp.asarray(0, jnp.int32)
        stat_max = lax.dynamic_update_slice(stat_max, row_max[:, :, 0].T, (zero_row, stat_col))
        stat_sum = lax.dynamic_update_slice(stat_sum, row_sum[:, :, 0].T, (zero_row, stat_col))
        stat_dot = lax.dynamic_update_slice(stat_dot, row_dot[:, :, 0].T, (zero_row, stat_col))
        return (
            query_grad,
            band_kgrad,
            band_vgrad,
            mem_kgrad,
            mem_vgrad,
            attn_rows,
            stat_max,
            stat_sum,
            stat_dot,
        )

    init = (
        jnp.zeros((tokens, width), jnp.float32),
        jnp.zeros((W + tokens, width), jnp.float32),
        jnp.zeros((W + tokens, width), jnp.float32),
        jnp.zeros((slot_total, width), jnp.float32),
        jnp.zeros((slot_total, width), jnp.float32),
        jnp.zeros((tokens, width), jnp.bfloat16),
        jnp.zeros((W, heads_total), jnp.float32),
        jnp.zeros((W, heads_total), jnp.float32),
        jnp.zeros((W, heads_total), jnp.float32),
    )
    (
        query_grad,
        band_kgrad,
        band_vgrad,
        mem_kgrad,
        mem_vgrad,
        attn_rows,
        stat_max,
        stat_sum,
        stat_dot,
    ) = lax.fori_loop(0, pair_count, pair_step, init)
    own_kgrad = band_kgrad[W:]
    own_vgrad = band_vgrad[W:]
    back_kgrad, back_vgrad = (
        passed_along(band_kgrad[:W].astype(jnp.bfloat16), "ctx", -1).astype(jnp.float32),
        passed_along(band_vgrad[:W].astype(jnp.bfloat16), "ctx", -1).astype(jnp.float32),
    )
    own_kgrad = own_kgrad.at[tokens - W :].add(back_kgrad)
    own_vgrad = own_vgrad.at[tokens - W :].add(back_vgrad)
    got_kgrad, got_vgrad = (
        lax.psum_scatter(
            mem_kgrad.astype(jnp.bfloat16), "ctx", scatter_dimension=0, tiled=True
        ).astype(jnp.float32),
        lax.psum_scatter(
            mem_vgrad.astype(jnp.bfloat16), "ctx", scatter_dimension=0, tiled=True
        ).astype(jnp.float32),
    )
    own_kgrad = own_kgrad.at[own_slots].add(got_kgrad)
    own_vgrad = own_vgrad.at[own_slots].add(got_vgrad)
    weight_part = lax.dot_general(
        attn_rows, grad_out, (((0,), (0,)), ((), ())), preferred_element_type=jnp.float32
    )
    weight_total = lax.psum(weight_part, ("fam", "ctx"))
    weight_grad = weight_total * (lax.axis_size("fam") * ctx_size * tokens) ** (-0.5)
    return (
        query_grad.astype(jnp.bfloat16)[None],
        own_kgrad.astype(jnp.bfloat16)[None],
        own_vgrad.astype(jnp.bfloat16)[None],
        weight_grad,
    )


def solution(mesh):
    return jax.shard_map(
        per_device,
        mesh=mesh,
        in_specs=(
            P("fam", "ctx", None),
            P("fam", "ctx", None),
            P("fam", "ctx", None),
            P("fam", "ctx", None),
            P(),
            P("fam", None),
            P("fam", None),
            P("fam", None),
        ),
        out_specs=(P("fam", "ctx", None), P("fam", "ctx", None), P("fam", "ctx", None), P()),
        check_vma=False,
    )
```

profile of v0, /device:TPU:1, one launch (start us, length us, event | category | flops | bytes accessed | tf_op | source)
XLA Modules:
  0.0 967.8 jit_solution(17995845950725439622)
XLA Ops:
  44.0 19.9 %all-gather.7.cloned.1.call-done = bf16[512,1024]{1,0:T(8,128)(2,1)} async-done(((bf16[16,1024]{1,0:T(8,128)(2,1)}), bf16[512,1024]{1,0:T(8,128)(2,1)}) %all-gather.7.cloned.1.call-update) | async-done | bytes 1048592 | tf_op jit(solution)/shard_map/all_gather | solution.py:108
  63.9 44.9 %all-gather.5.cloned.1.call-done = bf16[512,1024]{1,0:T(8,128)(2,1)} async-done(((bf16[16,1024]{1,0:T(8,128)(2,1)}), bf16[512,1024]{1,0:T(8,128)(2,1)}) %all-gather.5.cloned.1.call-update) | async-done | bytes 1048592 | tf_op jit(solution)/shard_map/all_gather | solution.py:107
  118.0 518.4 %while.27 = (s32[]{:T(128)}, bf16[512,1024]{1,0:T(8,128)(2,1)}, f32[1024,1024]{1,0:T(8,128)}, f32[1024,1024]{1,0:T(8,128)}, f32[512,1024]{1,0:T(8,128)}, /*index...) while((s32[]{:T(128)}, bf16[512,1024]{1,0:T(8,128)(2,1)}, ...), condition=%wide.region_14.15_spmd, body=%wide.region_10.14_spmd.sunk | while | flops 1247747584 | bytes 80244984 | solution.py:200
  144.4 13.6 %fusion.101 = bf16[2,64,512]{2,1,0:T(8,128)(2,1)S(1)} fusion(f32[2,512,1536]{2,1,0:T(8,128)} %fusion.99, bf16[512,2,64]{0,2,1:T(8,128)(2,1)S(1)} %bitcast.109, bf16[1024,2,64]{0,2,1:T(8,128)(2,1)S(1)} %bitcast.104, f32[2,512,1536]{2,1,0:T(8,128)} %get-tuple-element.467, f32[2,512]{1,0:T(2,128)S(1)} %broadcast_maximum_fusion.2), kind=kOutput, calls=%fused_computation.16.clone.1 | convolution fusion | flops 213125632 | bytes 13111296 | tf_op jit(solution)/shard_map/while/body/eval_jaxpr/gqk,kge->qge/dot_general | solution.py:75
  157.9 13.2 %fusion.102 = f32[1536,2,64]{0,2,1:T(8,128)S(1)} fusion(bf16[512,2,64]{0,2,1:T(8,128)(2,1)S(1)} %bitcast.107, f32[2,512,1536]{2,1,0:T(8,128)} %fusion.99, f32[2,512,1536]{2,1,0:T(8,128)} %get-tuple-element.467, f32[2,512]{1,0:T(2,128)S(1)} %broadcast_maximum_fusion.2), kind=kOutput, calls=%fused_computation.18.clone.1 | convolution fusion | flops 212339200 | bytes 13504512 | tf_op jit(solution)/shard_map/while/body/eval_jaxpr/gqk,qge->kge/dot_general | solution.py:76
  209.2 13.6 %fusion.101 = bf16[2,64,512]{2,1,0:T(8,128)(2,1)S(1)} fusion(f32[2,512,1536]{2,1,0:T(8,128)} %fusion.99, bf16[512,2,64]{0,2,1:T(8,128)(2,1)S(1)} %bitcast.109, bf16[1024,2,64]{0,2,1:T(8,128)(2,1)S(1)} %bitcast.104, f32[2,512,1536]{2,1,0:T(8,128)} %get-tuple-element.467, f32[2,512]{1,0:T(2,128)S(1)} %broadcast_maximum_fusion.2), kind=kOutput, calls=%fused_computation.16.clone.1 | convolution fusion | flops 213125632 | bytes 13111296 | tf_op jit(solution)/shard_map/while/body/eval_jaxpr/gqk,kge->qge/dot_general | solution.py:75
  222.7 13.2 %fusion.102 = f32[1536,2,64]{0,2,1:T(8,128)S(1)} fusion(bf16[512,2,64]{0,2,1:T(8,128)(2,1)S(1)} %bitcast.107, f32[2,512,1536]{2,1,0:T(8,128)} %fusion.99, f32[2,512,1536]{2,1,0:T(8,128)} %get-tuple-element.467, f32[2,512]{1,0:T(2,128)S(1)} %broadcast_maximum_fusion.2), kind=kOutput, calls=%fused_computation.18.clone.1 | convolution fusion | flops 212339200 | bytes 13504512 | tf_op jit(solution)/shard_map/while/body/eval_jaxpr/gqk,qge->kge/dot_general | solution.py:76
  274.0 13.6 %fusion.101 = bf16[2,64,512]{2,1,0:T(8,128)(2,1)S(1)} fusion(f32[2,512,1536]{2,1,0:T(8,128)} %fusion.99, bf16[512,2,64]{0,2,1:T(8,128)(2,1)S(1)} %bitcast.109, bf16[1024,2,64]{0,2,1:T(8,128)(2,1)S(1)} %bitcast.104, f32[2,512,1536]{2,1,0:T(8,128)} %get-tuple-element.467, f32[2,512]{1,0:T(2,128)S(1)} %broadcast_maximum_fusion.2), kind=kOutput, calls=%fused_computation.16.clone.1 | convolution fusion | flops 213125632 | bytes 13111296 | tf_op jit(solution)/shard_map/while/body/eval_jaxpr/gqk,kge->qge/dot_general | solution.py:75
  287.5 13.2 %fusion.102 = f32[1536,2,64]{0,2,1:T(8,128)S(1)} fusion(bf16[512,2,64]{0,2,1:T(8,128)(2,1)S(1)} %bitcast.107, f32[2,512,1536]{2,1,0:T(8,128)} %fusion.99, f32[2,512,1536]{2,1,0:T(8,128)} %get-tuple-element.467, f32[2,512]{1,0:T(2,128)S(1)} %broadcast_maximum_fusion.2), kind=kOutput, calls=%fused_computation.18.clone.1 | convolution fusion | flops 212339200 | bytes 13504512 | tf_op jit(solution)/shard_map/while/body/eval_jaxpr/gqk,qge->kge/dot_general | solution.py:76
  338.8 13.6 %fusion.101 = bf16[2,64,512]{2,1,0:T(8,128)(2,1)S(1)} fusion(f32[2,512,1536]{2,1,0:T(8,128)} %fusion.99, bf16[512,2,64]{0,2,1:T(8,128)(2,1)S(1)} %bitcast.109, bf16[1024,2,64]{0,2,1:T(8,128)(2,1)S(1)} %bitcast.104, f32[2,512,1536]{2,1,0:T(8,128)} %get-tuple-element.467, f32[2,512]{1,0:T(2,128)S(1)} %broadcast_maximum_fusion.2), kind=kOutput, calls=%fused_computation.16.clone.1 | convolution fusion | flops 213125632 | bytes 13111296 | tf_op jit(solution)/shard_map/while/body/eval_jaxpr/gqk,kge->qge/dot_general | solution.py:75
  352.4 13.2 %fusion.102 = f32[1536,2,64]{0,2,1:T(8,128)S(1)} fusion(bf16[512,2,64]{0,2,1:T(8,128)(2,1)S(1)} %bitcast.107, f32[2,512,1536]{2,1,0:T(8,128)} %fusion.99, f32[2,512,1536]{2,1,0:T(8,128)} %get-tuple-element.467, f32[2,512]{1,0:T(2,128)S(1)} %broadcast_maximum_fusion.2), kind=kOutput, calls=%fused_computation.18.clone.1 | convolution fusion | flops 212339200 | bytes 13504512 | tf_op jit(solution)/shard_map/while/body/eval_jaxpr/gqk,qge->kge/dot_general | solution.py:76
  403.6 13.6 %fusion.101 = bf16[2,64,512]{2,1,0:T(8,128)(2,1)S(1)} fusion(f32[2,512,1536]{2,1,0:T(8,128)} %fusion.99, bf16[512,2,64]{0,2,1:T(8,128)(2,1)S(1)} %bitcast.109, bf16[1024,2,64]{0,2,1:T(8,128)(2,1)S(1)} %bitcast.104, f32[2,512,1536]{2,1,0:T(8,128)} %get-tuple-element.467, f32[2,512]{1,0:T(2,128)S(1)} %broadcast_maximum_fusion.2), kind=kOutput, calls=%fused_computation.16.clone.1 | convolution fusion | flops 213125632 | bytes 13111296 | tf_op jit(solution)/shard_map/while/body/eval_jaxpr/gqk,kge->qge/dot_general | solution.py:75
  417.2 13.2 %fusion.102 = f32[1536,2,64]{0,2,1:T(8,128)S(1)} fusion(bf16[512,2,64]{0,2,1:T(8,128)(2,1)S(1)} %bitcast.107, f32[2,512,1536]{2,1,0:T(8,128)} %fusion.99, f32[2,512,1536]{2,1,0:T(8,128)} %get-tuple-element.467, f32[2,512]{1,0:T(2,128)S(1)} %broadcast_maximum_fusion.2), kind=kOutput, calls=%fused_computation.18.clone.1 | convolution fusion | flops 212339200 | bytes 13504512 | tf_op jit(solution)/shard_map/while/body/eval_jaxpr/gqk,qge->kge/dot_general | solution.py:76
  468.4 13.6 %fusion.101 = bf16[2,64,512]{2,1,0:T(8,128)(2,1)S(1)} fusion(f32[2,512,1536]{2,1,0:T(8,128)} %fusion.99, bf16[512,2,64]{0,2,1:T(8,128)(2,1)S(1)} %bitcast.109, bf16[1024,2,64]{0,2,1:T(8,128)(2,1)S(1)} %bitcast.104, f32[2,512,1536]{2,1,0:T(8,128)} %get-tuple-element.467, f32[2,512]{1,0:T(2,128)S(1)} %broadcast_maximum_fusion.2), kind=kOutput, calls=%fused_computation.16.clone.1 | convolution fusion | flops 213125632 | bytes 13111296 | tf_op jit(solution)/shard_map/while/body/eval_jaxpr/gqk,kge->qge/dot_general | solution.py:75
  482.0 13.2 %fusion.102 = f32[1536,2,64]{0,2,1:T(8,128)S(1)} fusion(bf16[512,2,64]{0,2,1:T(8,128)(2,1)S(1)} %bitcast.107, f32[2,512,1536]{2,1,0:T(8,128)} %fusion.99, f32[2,512,1536]{2,1,0:T(8,128)} %get-tuple-element.467, f32[2,512]{1,0:T(2,128)S(1)} %broadcast_maximum_fusion.2), kind=kOutput, calls=%fused_computation.18.clone.1 | convolution fusion | flops 212339200 | bytes 13504512 | tf_op jit(solution)/shard_map/while/body/eval_jaxpr/gqk,qge->kge/dot_general | solution.py:76
  521.6 7.0 fusion.100
  533.2 13.6 %fusion.101 = bf16[2,64,512]{2,1,0:T(8,128)(2,1)S(1)} fusion(f32[2,512,1536]{2,1,0:T(8,128)} %fusion.99, bf16[512,2,64]{0,2,1:T(8,128)(2,1)S(1)} %bitcast.109, bf16[1024,2,64]{0,2,1:T(8,128)(2,1)S(1)} %bitcast.104, f32[2,512,1536]{2,1,0:T(8,128)} %get-tuple-element.467, f32[2,512]{1,0:T(2,128)S(1)} %broadcast_maximum_fusion.2), kind=kOutput, calls=%fused_computation.16.clone.1 | convolution fusion | flops 213125632 | bytes 13111296 | tf_op jit(solution)/shard_map/while/body/eval_jaxpr/gqk,kge->qge/dot_general | solution.py:75
  546.8 13.2 %fusion.102 = f32[1536,2,64]{0,2,1:T(8,128)S(1)} fusion(bf16[512,2,64]{0,2,1:T(8,128)(2,1)S(1)} %bitcast.107, f32[2,512,1536]{2,1,0:T(8,128)} %fusion.99, f32[2,512,1536]{2,1,0:T(8,128)} %get-tuple-element.467, f32[2,512]{1,0:T(2,128)S(1)} %broadcast_maximum_fusion.2), kind=kOutput, calls=%fused_computation.18.clone.1 | convolution fusion | flops 212339200 | bytes 13504512 | tf_op jit(solution)/shard_map/while/body/eval_jaxpr/gqk,qge->kge/dot_general | solution.py:76
  598.0 13.6 %fusion.101 = bf16[2,64,512]{2,1,0:T(8,128)(2,1)S(1)} fusion(f32[2,512,1536]{2,1,0:T(8,128)} %fusion.99, bf16[512,2,64]{0,2,1:T(8,128)(2,1)S(1)} %bitcast.109, bf16[1024,2,64]{0,2,1:T(8,128)(2,1)S(1)} %bitcast.104, f32[2,512,1536]{2,1,0:T(8,128)} %get-tuple-element.467, f32[2,512]{1,0:T(2,128)S(1)} %broadcast_maximum_fusion.2), kind=kOutput, calls=%fused_computation.16.clone.1 | convolution fusion | flops 213125632 | bytes 13111296 | tf_op jit(solution)/shard_map/while/body/eval_jaxpr/gqk,kge->qge/dot_general | solution.py:75
  611.6 13.2 %fusion.102 = f32[1536,2,64]{0,2,1:T(8,128)S(1)} fusion(bf16[512,2,64]{0,2,1:T(8,128)(2,1)S(1)} %bitcast.107, f32[2,512,1536]{2,1,0:T(8,128)} %fusion.99, f32[2,512,1536]{2,1,0:T(8,128)} %get-tuple-element.467, f32[2,512]{1,0:T(2,128)S(1)} %broadcast_maximum_fusion.2), kind=kOutput, calls=%fused_computation.18.clone.1 | convolution fusion | flops 212339200 | bytes 13504512 | tf_op jit(solution)/shard_map/while/body/eval_jaxpr/gqk,qge->kge/dot_general | solution.py:76
  660.6 9.2 collective-permute-done.2
  671.4 43.8 %reduce-scatter.5.cloned.1.call-done = bf16[16,1024]{1,0:T(8,128)(2,1)} async-done(((bf16[512,1024]{1,0:T(8,128)(2,1)}), bf16[16,1024]{1,0:T(8,128)(2,1)}) %reduce-scatter.5.cloned.1.call-update) | async-done | bytes 32784 | tf_op jit(solution)/shard_map/reduce_scatter | solution.py:213
  716.9 79.4 %reduce-scatter.3.cloned.1.call-done = bf16[16,1024]{1,0:T(8,128)(2,1)} async-done(((bf16[512,1024]{1,0:T(8,128)(2,1)}), bf16[16,1024]{1,0:T(8,128)(2,1)}) %reduce-scatter.3.cloned.1.call-update) | async-done | bytes 32784 | tf_op jit(solution)/shard_map/reduce_scatter | solution.py:210
  804.2 152.1 %all-reduce.2.cloned.1.call-done = f32[1024,1024]{1,0:T(8,128)} async-done(((f32[1024,1024]{1,0:T(8,128)}), f32[1024,1024]{1,0:T(8,128)}) %all-reduce.2.cloned.1.call-update) | async-done | bytes 4194320 | tf_op jit(solution)/shard_map/psum | solution.py:222
  (403 shorter events, 382.4 us)
Async XLA Ops:
  7.2 22.5 %copy-start = (bf16[1024,1024]{1,0:T(8,128)(2,1)S(1)}, bf16[1024,1024]{1,0:T(8,128)(2,1)}, u32[]{:S(2)}) copy-start(bf16[1024,1024]{1,0:T(8,128)(2,1)} %param.22) | copy-start | bytes 6291460
  7.2 56.7 %all-gather.7.cloned.1.call-start = ((), (), s32[]{:S(2)}) async-start(), calls=%async_computation.6 | async-start | bytes 1081344 | tf_op jit(solution)/shard_map/all_gather | solution.py:108
  8.1 0.5 copy-start.6
  11.2 97.5 %all-gather.5.cloned.1.call-start = ((), (), s32[]{:S(2)}) async-start(), calls=%async_computation.5 | async-start | bytes 1081344 | tf_op jit(solution)/shard_map/all_gather | solution.py:107
  11.3 31.3 %collective-permute-start.1 = (bf16[512,1024]{1,0:T(8,128)(2,1)}, bf16[512,1024]{1,0:T(8,128)(2,1)S(1)}, u32[]{:S(2)}, u32[]{:S(2)}) collective-permute-start(bf16[512,1024]{1,0:T(8,128)(2,1)} %bitcast.115), channel_id=1, source_target_pairs={{0,1},{1,2},{2,3},{3,4},{4,5},{5,6},{6,7},{7,8},{8,9},{9,10},{10,1... | collective-permute-start | bytes 3145736 | tf_op jit(solution)/shard_map/ppermute | solution.py:15
  15.9 23.8 %collective-permute-start = (bf16[512,1024]{1,0:T(8,128)(2,1)}, bf16[512,1024]{1,0:T(8,128)(2,1)}, u32[]{:S(2)}, u32[]{:S(2)}) collective-permute-start(bf16[512,1024]{1,0:T(8,128)(2,1)} %bitcast.111), channel_id=1, source_target_pairs={{0,1},{1,2},{2,3},{3,4},{4,5},{5,6},{6,7},{7,8},{8,9},{9,10},{10,1... | collective-permute-start | bytes 3145736 | tf_op jit(solution)/shard_map/ppermute | solution.py:15
  20.4 694.8 %reduce-scatter.5.cloned.1.call-start = ((), (), s32[]{:S(2)}) async-start(), calls=%async_computation.3 | async-start | bytes 1081344 | tf_op jit(solution)/shard_map/reduce_scatter | solution.py:213
  29.7 10.0 %copy-start.4 = (bf16[1,512,1024]{2,1,0:T(8,128)(2,1)S(1)}, bf16[1,512,1024]{2,1,0:T(8,128)(2,1)}, u32[]{:S(2)}) copy-start(bf16[1,512,1024]{2,1,0:T(8,128)(2,1)} %param.19) | copy-start | bytes 3145732
  33.3 9.3 copy-start.5
  636.4 3.1 copy-start.3
  639.4 156.9 %reduce-scatter.3.cloned.1.call-start = ((), (), s32[]{:S(2)}) async-start(), calls=%async_computation.2 | async-start | bytes 1081344 | tf_op jit(solution)/shard_map/reduce_scatter | solution.py:210
  640.7 315.6 %all-reduce.2.cloned.1.call-start = ((), (), s32[]{:S(2)}) async-start(), calls=%async_computation.4 | async-start | bytes 8388608 | tf_op jit(solution)/shard_map/psum | solution.py:222
  642.5 16.1 %collective-permute-start.3 = (bf16[512,1024]{1,0:T(8,128)(2,1)S(1)}, bf16[512,1024]{1,0:T(8,128)(2,1)S(1)}, u32[]{:S(2)}, u32[]{:S(2)}) collective-permute-start(bf16[512,1024]{1,0:T(8,128)(2,1)S(1)} %slice.88), channel_id=1, source_target_pairs={{1,0},{2,1},{3,2},{4,3},{5,4},{6,5},{7,6},{8,7},{9,8},{10,9},{11,1... | collective-permute-start | bytes 3145736 | tf_op jit(solution)/shard_map/ppermute | solution.py:15
  649.6 20.2 %copy-start.2 = (f32[1024,1024]{1,0:T(8,128)S(1)}, f32[1024,1024]{1,0:T(8,128)}, u32[]{:S(2)}) copy-start(f32[1024,1024]{1,0:T(8,128)} %get-tuple-element.279) | copy-start | bytes 12582916
  651.6 18.3 %collective-permute-start.2 = (bf16[512,1024]{1,0:T(8,128)(2,1)S(1)}, bf16[512,1024]{1,0:T(8,128)(2,1)S(1)}, u32[]{:S(2)}, u32[]{:S(2)}) collective-permute-start(bf16[512,1024]{1,0:T(8,128)(2,1)S(1)} %slice.89), channel_id=1, source_target_pairs={{1,0},{2,1},{3,2},{4,3},{5,4},{6,5},{7,6},{8,7},{9,8},{10,9},{11,1... | collective-permute-start | bytes 3145736 | tf_op jit(solution)/shard_map/ppermute | solution.py:15
  801.3 160.0 %copy-start.1 = (bf16[1024,1024]{1,0:T(8,128)(2,1)S(1)}, bf16[1024,1024]{1,0:T(8,128)(2,1)}, u32[]{:S(2)}) copy-start(bf16[1024,1024]{1,0:T(8,128)(2,1)} %param.22) | copy-start | bytes 6291460
Sparse Core Ops, SparseCore 0:
  11.4 52.4 all-gather.6
  66.7 41.9 all-gather.4
  639.6 75.6 reduce-scatter.4
  719.5 76.7 reduce-scatter.2
  801.1 155.0 all-reduce.1
where the time goes:
time: 972 us; the launch traced here: 968 us
  matrix products  379 us (39%)
  waiting for transfers between devices  361 us (37%)
  local copies, waits for them, and re-layouts  166 us (17%)
  other arithmetic  35.4 us (4%)
  between operations  13.9 us (1%)
  starting transfers between devices  11.1 us (1%)
    psum x1, waiting for transfers between devices, per_device(): weight_total = lax.psum(weight_part, ('fam', 'ctx'))  152 us
    dot_general x8, matrix products, attend(): jnp.einsum('gqk,kge->qge', grad_score, key_blk, preferred_element_type=jn...  108 us
    dot_general x8, matrix products, attend(): jnp.einsum('gqk,qge->kge', grad_score, query_blk, preferred_element_type=...  105 us
    reduce_scatter x1, waiting for transfers between devices, per_device(): lax.psum_scatter(mem_kgrad.astype(jnp.bfloat16), 'ctx', scatter_dimension...  79.4 us
    sub x8, matrix products, attend(): expo = jnp.where(live, jnp.exp(shifted - row_max), 0.0)  56 us
    dynamic_slice x88, local copies, waits for them, and re-layouts, columns_of(): return lax.dynamic_slice_in_dim(array, column, span, 1)  50 us
    all_gather x1, waiting for transfers between devices, per_device(): lax.all_gather(key_loc[own_slots], 'ctx', axis=0, tiled=True)  44.9 us
    reduce_scatter x1, waiting for transfers between devices, per_device(): lax.psum_scatter(mem_vgrad.astype(jnp.bfloat16), 'ctx', scatter_dimension...  43.8 us
  transfers between devices with their start and end apart: 9, of which 8 were waited for; matrix products, arithmetic and copies ran while one was open for 4% of the time, Pallas kernels for 0%

commit v1 on v0

--- a/solution.py
+++ b/solution.py
@@ -7,6 +7,18 @@
 W = 512
 BLK = 128
 NEG_FILL = -1e30
+
+
+def convert_state(t0):
+    return jnp.concatenate(
+        lax.all_to_all(
+            jnp.stack([t0 for _ in range(lax.axis_size("ctx"))]),
+            axis_name="ctx",
+            split_axis=0,
+            concat_axis=0,
+        ),
+        axis=0,
+    )
 
 
 def passed_along(value, axis, steps):
@@ -104,7 +116,7 @@
     mem_info = token_info(source, tables)
     own_slots = lax.dynamic_slice_in_dim(slots, ctx_index * slot_dev, slot_dev)
     mem_keys, mem_values = (
-        lax.all_gather(key_loc[own_slots], "ctx", axis=0, tiled=True),
+        convert_state(key_loc[own_slots]),
         lax.all_gather(value_loc[own_slots], "ctx", axis=0, tiled=True),
     )
     halo_keys, halo_values = passed_along((key_loc, value_loc), "ctx", 1)

time: 972 us -> 938 us (0.965)
  waiting for transfers between devices: 361 us -> 315 us
    all_gather x1 -> x0, waiting for transfers between devices: 44.9 us -> none  [per_device(): lax.all_gather(key_loc[own_slots], 'ctx', axis=0, tiled=True)]
  transfers between devices with their start and end apart: 9 -> 9, of which waited for: 8 -> 8; matrix products, arithmetic and copies ran while one was open for 4% -> 5% of each run, Pallas kernels for 0% -> 0%
where the time goes in v1:
time: 938 us; the launch traced here: 933 us
  matrix products  379 us (40%)
  waiting for transfers between devices  315 us (34%)
  local copies, waits for them, and re-layouts  167 us (18%)
  other arithmetic  37.6 us (4%)
  starting transfers between devices  18.5 us (2%)
  between operations  14 us (1%)
    psum x1, waiting for transfers between devices, per_device(): weight_total = lax.psum(weight_part, ('fam', 'ctx'))  152 us
    dot_general x8, matrix products, attend(): jnp.einsum('gqk,kge->qge', grad_score, key_blk, preferred_element_type=jn...  108 us
    dot_general x8, matrix products, attend(): jnp.einsum('gqk,qge->kge', grad_score, query_blk, preferred_element_type=...  105 us
    reduce_scatter x1, waiting for transfers between devices, per_device(): lax.psum_scatter(mem_kgrad.astype(jnp.bfloat16), 'ctx', scatter_dimension...  79.5 us
    sub x8, matrix products, attend(): expo = jnp.where(live, jnp.exp(shifted - row_max), 0.0)  56 us
    dynamic_slice x88, local copies, waits for them, and re-layouts, columns_of(): return lax.dynamic_slice_in_dim(array, column, span, 1)  51 us
    reduce_scatter x1, waiting for transfers between devices, per_device(): lax.psum_scatter(mem_vgrad.astype(jnp.bfloat16), 'ctx', scatter_dimension...  43.7 us
    dynamic_slice x64, local copies, waits for them, and re-layouts, add_into(): current = lax.dynamic_slice(target, (row_index, column), update.shape)  38.1 us
  transfers between devices with their start and end apart: 9, of which 8 were waited for; matrix products, arithmetic and copies ran while one was open for 5% of the time, Pallas kernels for 0%

profile of v1, /device:TPU:1, one launch (start us, length us, event | category | flops | bytes accessed | tf_op | source)
XLA Modules:
  0.0 933.3 jit_solution(17905807958382159702)
XLA Ops:
  20.3 7.3 all-to-all-start
  52.5 20.4 %all-gather.3.cloned.1.call-done = bf16[512,1024]{1,0:T(8,128)(2,1)} async-done(((bf16[16,1024]{1,0:T(8,128)(2,1)}), bf16[512,1024]{1,0:T(8,128)(2,1)}) %all-gather.3.cloned.1.call-update) | async-done | bytes 1048592 | tf_op jit(solution)/shard_map/all_gather | solution.py:120
  82.1 519.6 %while.27 = (s32[]{:T(128)}, bf16[512,1024]{1,0:T(8,128)(2,1)}, f32[1024,1024]{1,0:T(8,128)}, f32[1024,1024]{1,0:T(8,128)}, f32[512,1024]{1,0:T(8,128)}, /*index...) while((s32[]{:T(128)}, bf16[512,1024]{1,0:T(8,128)(2,1)}, ...), condition=%wide.region_14.15_spmd, body=%wide.region_10.14_spmd.sunk | while | flops 1247747584 | bytes 88633648 | solution.py:212
  97.1 7.0 fusion.100
  108.6 13.6 %fusion.101 = bf16[2,64,512]{2,1,0:T(8,128)(2,1)S(1)} fusion(f32[2,512,1536]{2,1,0:T(8,128)} %fusion.99, bf16[512,2,64]{0,2,1:T(8,128)(2,1)S(1)} %bitcast.110, bf16[1024,2,64]{0,2,1:T(8,128)(2,1)S(1)} %bitcast.105, f32[2,512,1536]{2,1,0:T(8,128)} %get-tuple-element.467, f32[2,512]{1,0:T(2,128)S(1)} %broadcast_maximum_fusion.2), kind=kOutput, calls=%fused_computation.16.clone.1 | convolution fusion | flops 213125632 | bytes 13111296 | tf_op jit(solution)/shard_map/while/body/eval_jaxpr/gqk,kge->qge/dot_general | solution.py:87
  122.2 13.2 %fusion.102 = f32[1536,2,64]{0,2,1:T(8,128)S(1)} fusion(bf16[512,2,64]{0,2,1:T(8,128)(2,1)S(1)} %bitcast.108, f32[2,512,1536]{2,1,0:T(8,128)} %fusion.99, f32[2,512,1536]{2,1,0:T(8,128)} %get-tuple-element.467, f32[2,512]{1,0:T(2,128)S(1)} %broadcast_maximum_fusion.2), kind=kOutput, calls=%fused_computation.18.clone.1 | convolution fusion | flops 212339200 | bytes 13504512 | tf_op jit(solution)/shard_map/while/body/eval_jaxpr/gqk,qge->kge/dot_general | solution.py:88
  173.6 13.6 %fusion.101 = bf16[2,64,512]{2,1,0:T(8,128)(2,1)S(1)} fusion(f32[2,512,1536]{2,1,0:T(8,128)} %fusion.99, bf16[512,2,64]{0,2,1:T(8,128)(2,1)S(1)} %bitcast.110, bf16[1024,2,64]{0,2,1:T(8,128)(2,1)S(1)} %bitcast.105, f32[2,512,1536]{2,1,0:T(8,128)} %get-tuple-element.467, f32[2,512]{1,0:T(2,128)S(1)} %broadcast_maximum_fusion.2), kind=kOutput, calls=%fused_computation.16.clone.1 | convolution fusion | flops 213125632 | bytes 13111296 | tf_op jit(solution)/shard_map/while/body/eval_jaxpr/gqk,kge->qge/dot_general | solution.py:87
  187.2 13.2 %fusion.102 = f32[1536,2,64]{0,2,1:T(8,128)S(1)} fusion(bf16[512,2,64]{0,2,1:T(8,128)(2,1)S(1)} %bitcast.108, f32[2,512,1536]{2,1,0:T(8,128)} %fusion.99, f32[2,512,1536]{2,1,0:T(8,128)} %get-tuple-element.467, f32[2,512]{1,0:T(2,128)S(1)} %broadcast_maximum_fusion.2), kind=kOutput, calls=%fused_computation.18.clone.1 | convolution fusion | flops 212339200 | bytes 13504512 | tf_op jit(solution)/shard_map/while/body/eval_jaxpr/gqk,qge->kge/dot_general | solution.py:88
  238.6 13.6 %fusion.101 = bf16[2,64,512]{2,1,0:T(8,128)(2,1)S(1)} fusion(f32[2,512,1536]{2,1,0:T(8,128)} %fusion.99, bf16[512,2,64]{0,2,1:T(8,128)(2,1)S(1)} %bitcast.110, bf16[1024,2,64]{0,2,1:T(8,128)(2,1)S(1)} %bitcast.105, f32[2,512,1536]{2,1,0:T(8,128)} %get-tuple-element.467, f32[2,512]{1,0:T(2,128)S(1)} %broadcast_maximum_fusion.2), kind=kOutput, calls=%fused_computation.16.clone.1 | convolution fusion | flops 213125632 | bytes 13111296 | tf_op jit(solution)/shard_map/while/body/eval_jaxpr/gqk,kge->qge/dot_general | solution.py:87
  252.1 13.2 %fusion.102 = f32[1536,2,64]{0,2,1:T(8,128)S(1)} fusion(bf16[512,2,64]{0,2,1:T(8,128)(2,1)S(1)} %bitcast.108, f32[2,512,1536]{2,1,0:T(8,128)} %fusion.99, f32[2,512,1536]{2,1,0:T(8,128)} %get-tuple-element.467, f32[2,512]{1,0:T(2,128)S(1)} %broadcast_maximum_fusion.2), kind=kOutput, calls=%fused_computation.18.clone.1 | convolution fusion | flops 212339200 | bytes 13504512 | tf_op jit(solution)/shard_map/while/body/eval_jaxpr/gqk,qge->kge/dot_general | solution.py:88
  303.5 13.6 %fusion.101 = bf16[2,64,512]{2,1,0:T(8,128)(2,1)S(1)} fusion(f32[2,512,1536]{2,1,0:T(8,128)} %fusion.99, bf16[512,2,64]{0,2,1:T(8,128)(2,1)S(1)} %bitcast.110, bf16[1024,2,64]{0,2,1:T(8,128)(2,1)S(1)} %bitcast.105, f32[2,512,1536]{2,1,0:T(8,128)} %get-tuple-element.467, f32[2,512]{1,0:T(2,128)S(1)} %broadcast_maximum_fusion.2), kind=kOutput, calls=%fused_computation.16.clone.1 | convolution fusion | flops 213125632 | bytes 13111296 | tf_op jit(solution)/shard_map/while/body/eval_jaxpr/gqk,kge->qge/dot_general | solution.py:87
  317.1 13.2 %fusion.102 = f32[1536,2,64]{0,2,1:T(8,128)S(1)} fusion(bf16[512,2,64]{0,2,1:T(8,128)(2,1)S(1)} %bitcast.108, f32[2,512,1536]{2,1,0:T(8,128)} %fusion.99, f32[2,512,1536]{2,1,0:T(8,128)} %get-tuple-element.467, f32[2,512]{1,0:T(2,128)S(1)} %broadcast_maximum_fusion.2), kind=kOutput, calls=%fused_computation.18.clone.1 | convolution fusion | flops 212339200 | bytes 13504512 | tf_op jit(solution)/shard_map/while/body/eval_jaxpr/gqk,qge->kge/dot_general | solution.py:88
  368.5 13.6 %fusion.101 = bf16[2,64,512]{2,1,0:T(8,128)(2,1)S(1)} fusion(f32[2,512,1536]{2,1,0:T(8,128)} %fusion.99, bf16[512,2,64]{0,2,1:T(8,128)(2,1)S(1)} %bitcast.110, bf16[1024,2,64]{0,2,1:T(8,128)(2,1)S(1)} %bitcast.105, f32[2,512,1536]{2,1,0:T(8,128)} %get-tuple-element.467, f32[2,512]{1,0:T(2,128)S(1)} %broadcast_maximum_fusion.2), kind=kOutput, calls=%fused_computation.16.clone.1 | convolution fusion | flops 213125632 | bytes 13111296 | tf_op jit(solution)/shard_map/while/body/eval_jaxpr/gqk,kge->qge/dot_general | solution.py:87
  382.0 13.2 %fusion.102 = f32[1536,2,64]{0,2,1:T(8,128)S(1)} fusion(bf16[512,2,64]{0,2,1:T(8,128)(2,1)S(1)} %bitcast.108, f32[2,512,1536]{2,1,0:T(8,128)} %fusion.99, f32[2,512,1536]{2,1,0:T(8,128)} %get-tuple-element.467, f32[2,512]{1,0:T(2,128)S(1)} %broadcast_maximum_fusion.2), kind=kOutput, calls=%fused_computation.18.clone.1 | convolution fusion | flops 212339200 | bytes 13504512 | tf_op jit(solution)/shard_map/while/body/eval_jaxpr/gqk,qge->kge/dot_general | solution.py:88
  433.4 13.6 %fusion.101 = bf16[2,64,512]{2,1,0:T(8,128)(2,1)S(1)} fusion(f32[2,512,1536]{2,1,0:T(8,128)} %fusion.99, bf16[512,2,64]{0,2,1:T(8,128)(2,1)S(1)} %bitcast.110, bf16[1024,2,64]{0,2,1:T(8,128)(2,1)S(1)} %bitcast.105, f32[2,512,1536]{2,1,0:T(8,128)} %get-tuple-element.467, f32[2,512]{1,0:T(2,128)S(1)} %broadcast_maximum_fusion.2), kind=kOutput, calls=%fused_computation.16.clone.1 | convolution fusion | flops 213125632 | bytes 13111296 | tf_op jit(solution)/shard_map/while/body/eval_jaxpr/gqk,kge->qge/dot_general | solution.py:87
  447.0 13.2 %fusion.102 = f32[1536,2,64]{0,2,1:T(8,128)S(1)} fusion(bf16[512,2,64]{0,2,1:T(8,128)(2,1)S(1)} %bitcast.108, f32[2,512,1536]{2,1,0:T(8,128)} %fusion.99, f32[2,512,1536]{2,1,0:T(8,128)} %get-tuple-element.467, f32[2,512]{1,0:T(2,128)S(1)} %broadcast_maximum_fusion.2), kind=kOutput, calls=%fused_computation.18.clone.1 | convolution fusion | flops 212339200 | bytes 13504512 | tf_op jit(solution)/shard_map/while/body/eval_jaxpr/gqk,qge->kge/dot_general | solution.py:88
  498.3 13.6 %fusion.101 = bf16[2,64,512]{2,1,0:T(8,128)(2,1)S(1)} fusion(f32[2,512,1536]{2,1,0:T(8,128)} %fusion.99, bf16[512,2,64]{0,2,1:T(8,128)(2,1)S(1)} %bitcast.110, bf16[1024,2,64]{0,2,1:T(8,128)(2,1)S(1)} %bitcast.105, f32[2,512,1536]{2,1,0:T(8,128)} %get-tuple-element.467, f32[2,512]{1,0:T(2,128)S(1)} %broadcast_maximum_fusion.2), kind=kOutput, calls=%fused_computation.16.clone.1 | convolution fusion | flops 213125632 | bytes 13111296 | tf_op jit(solution)/shard_map/while/body/eval_jaxpr/gqk,kge->qge/dot_general | solution.py:87
  511.9 13.2 %fusion.102 = f32[1536,2,64]{0,2,1:T(8,128)S(1)} fusion(bf16[512,2,64]{0,2,1:T(8,128)(2,1)S(1)} %bitcast.108, f32[2,512,1536]{2,1,0:T(8,128)} %fusion.99, f32[2,512,1536]{2,1,0:T(8,128)} %get-tuple-element.467, f32[2,512]{1,0:T(2,128)S(1)} %broadcast_maximum_fusion.2), kind=kOutput, calls=%fused_computation.18.clone.1 | convolution fusion | flops 212339200 | bytes 13504512 | tf_op jit(solution)/shard_map/while/body/eval_jaxpr/gqk,qge->kge/dot_general | solution.py:88
  563.3 13.6 %fusion.101 = bf16[2,64,512]{2,1,0:T(8,128)(2,1)S(1)} fusion(f32[2,512,1536]{2,1,0:T(8,128)} %fusion.99, bf16[512,2,64]{0,2,1:T(8,128)(2,1)S(1)} %bitcast.110, bf16[1024,2,64]{0,2,1:T(8,128)(2,1)S(1)} %bitcast.105, f32[2,512,1536]{2,1,0:T(8,128)} %get-tuple-element.467, f32[2,512]{1,0:T(2,128)S(1)} %broadcast_maximum_fusion.2), kind=kOutput, calls=%fused_computation.16.clone.1 | convolution fusion | flops 213125632 | bytes 13111296 | tf_op jit(solution)/shard_map/while/body/eval_jaxpr/gqk,kge->qge/dot_general | solution.py:87
  576.8 13.2 %fusion.102 = f32[1536,2,64]{0,2,1:T(8,128)S(1)} fusion(bf16[512,2,64]{0,2,1:T(8,128)(2,1)S(1)} %bitcast.108, f32[2,512,1536]{2,1,0:T(8,128)} %fusion.99, f32[2,512,1536]{2,1,0:T(8,128)} %get-tuple-element.467, f32[2,512]{1,0:T(2,128)S(1)} %broadcast_maximum_fusion.2), kind=kOutput, calls=%fused_computation.18.clone.1 | convolution fusion | flops 212339200 | bytes 13504512 | tf_op jit(solution)/shard_map/while/body/eval_jaxpr/gqk,qge->kge/dot_general | solution.py:88
  625.9 9.2 collective-permute-done.2
  636.7 43.7 %reduce-scatter.5.cloned.1.call-done = bf16[16,1024]{1,0:T(8,128)(2,1)} async-done(((bf16[512,1024]{1,0:T(8,128)(2,1)}), bf16[16,1024]{1,0:T(8,128)(2,1)}) %reduce-scatter.5.cloned.1.call-update) | async-done | bytes 32784 | tf_op jit(solution)/shard_map/reduce_scatter | solution.py:225
  682.2 79.5 %reduce-scatter.3.cloned.1.call-done = bf16[16,1024]{1,0:T(8,128)(2,1)} async-done(((bf16[512,1024]{1,0:T(8,128)(2,1)}), bf16[16,1024]{1,0:T(8,128)(2,1)}) %reduce-scatter.3.cloned.1.call-update) | async-done | bytes 32784 | tf_op jit(solution)/shard_map/reduce_scatter | solution.py:222
  769.6 152.1 %all-reduce.2.cloned.1.call-done = f32[1024,1024]{1,0:T(8,128)} async-done(((f32[1024,1024]{1,0:T(8,128)}), f32[1024,1024]{1,0:T(8,128)}) %all-reduce.2.cloned.1.call-update) | async-done | bytes 4194320 | tf_op jit(solution)/shard_map/psum | solution.py:234
  (437 shorter events, 384.6 us)
Async XLA Ops:
  7.2 30.8 %copy-start = (bf16[1024,1024]{1,0:T(8,128)(2,1)S(1)}, bf16[1024,1024]{1,0:T(8,128)(2,1)}, u32[]{:S(2)}) copy-start(bf16[1024,1024]{1,0:T(8,128)(2,1)} %param.22) | copy-start | bytes 6291460
  7.2 25.1 %copy-start.8 = (s32[1,512]{1,0:T(1,128)S(1)}, s32[1,512]{1,0:T(1,128)}, u32[]{:S(2)}) copy-start(s32[1,512]{1,0:T(1,128)} %param.25) | copy-start | bytes 6148
  7.2 65.7 %all-gather.3.cloned.1.call-start = ((), (), s32[]{:S(2)}) async-start(), calls=%async_computation.6 | async-start | bytes 1081344 | tf_op jit(solution)/shard_map/all_gather | solution.py:120
  7.2 41.2 %collective-permute-start.1 = (bf16[512,1024]{1,0:T(8,128)(2,1)}, bf16[512,1024]{1,0:T(8,128)(2,1)}, u32[]{:S(2)}, u32[]{:S(2)}) collective-permute-start(bf16[512,1024]{1,0:T(8,128)(2,1)} %bitcast.116), channel_id=1, source_target_pairs={{0,1},{1,2},{2,3},{3,4},{4,5},{5,6},{6,7},{7,8},{8,9},{9,10},{10,1... | collective-permute-start | bytes 3145736 | tf_op jit(solution)/shard_map/ppermute | solution.py:27
  12.7 7.6 copy-start.9
  15.3 30.3 %collective-permute-start = (bf16[512,1024]{1,0:T(8,128)(2,1)}, bf16[512,1024]{1,0:T(8,128)(2,1)}, u32[]{:S(2)}, u32[]{:S(2)}) collective-permute-start(bf16[512,1024]{1,0:T(8,128)(2,1)} %bitcast.113), channel_id=1, source_target_pairs={{0,1},{1,2},{2,3},{3,4},{4,5},{5,6},{6,7},{7,8},{8,9},{9,10},{10,1... | collective-permute-start | bytes 3145736 | tf_op jit(solution)/shard_map/ppermute | solution.py:27
  20.3 32.1 %all-to-all-start = ((bf16[32,16,1024]{2,1,0:T(8,128)(2,1)}), bf16[32,16,1024]{2,1,0:T(8,128)(2,1)S(1)}, u32[]{:S(2)}, u32[]{:S(2)}) async-start(bf16[32,16,1024]{2,1,0:T(8,128)(2,1)} %stack.2), calls=%async_computation | async-start | bytes 2097152 | tf_op jit(solution)/shard_map/all_to_all | solution.py:14
  27.6 652.9 %reduce-scatter.5.cloned.1.call-start = ((), (), s32[]{:S(2)}) async-start(), calls=%async_computation.4 | async-start | bytes 1081344 | tf_op jit(solution)/shard_map/reduce_scatter | solution.py:225
  38.0 7.6 copy-start.6
  41.5 6.9 copy-start.7
  142.5 4.6 copy-start.5
  207.4 4.6 copy-start.5
  272.4 4.6 copy-start.5
  337.4 4.6 copy-start.5
  402.3 4.6 copy-start.5
  467.3 4.6 copy-start.5
  532.2 4.6 copy-start.5
  597.1 4.6 copy-start.5
  604.7 157.0 %reduce-scatter.3.cloned.1.call-start = ((), (), s32[]{:S(2)}) async-start(), calls=%async_computation.3 | async-start | bytes 1081344 | tf_op jit(solution)/shard_map/reduce_scatter | solution.py:222
  606.0 315.7 %all-reduce.2.cloned.1.call-start = ((), (), s32[]{:S(2)}) async-start(), calls=%async_computation.5 | async-start | bytes 8388608 | tf_op jit(solution)/shard_map/psum | solution.py:234
  607.8 16.1 %collective-permute-start.3 = (bf16[512,1024]{1,0:T(8,128)(2,1)S(1)}, bf16[512,1024]{1,0:T(8,128)(2,1)S(1)}, u32[]{:S(2)}, u32[]{:S(2)}) collective-permute-start(bf16[512,1024]{1,0:T(8,128)(2,1)S(1)} %slice.88), channel_id=1, source_target_pairs={{1,0},{2,1},{3,2},{4,3},{5,4},{6,5},{7,6},{8,7},{9,8},{10,9},{11,1... | collective-permute-start | bytes 3145736 | tf_op jit(solution)/shard_map/ppermute | solution.py:27
  614.9 20.2 %copy-start.2 = (f32[1024,1024]{1,0:T(8,128)S(1)}, f32[1024,1024]{1,0:T(8,128)}, u32[]{:S(2)}) copy-start(f32[1024,1024]{1,0:T(8,128)} %get-tuple-element.279) | copy-start | bytes 12582916
  616.9 18.3 %collective-permute-start.2 = (bf16[512,1024]{1,0:T(8,128)(2,1)S(1)}, bf16[512,1024]{1,0:T(8,128)(2,1)S(1)}, u32[]{:S(2)}, u32[]{:S(2)}) collective-permute-start(bf16[512,1024]{1,0:T(8,128)(2,1)S(1)} %slice.89), channel_id=1, source_target_pairs={{1,0},{2,1},{3,2},{4,3},{5,4},{6,5},{7,6},{8,7},{9,8},{10,9},{11,1... | collective-permute-start | bytes 3145736 | tf_op jit(solution)/shard_map/ppermute | solution.py:27
  766.7 160.0 %copy-start.1 = (bf16[1024,1024]{1,0:T(8,128)(2,1)S(1)}, bf16[1024,1024]{1,0:T(8,128)(2,1)}, u32[]{:S(2)}) copy-start(bf16[1024,1024]{1,0:T(8,128)(2,1)} %param.22) | copy-start | bytes 6291460
  (9 other events, 20.7 us)
Sparse Core Ops, SparseCore 0:
  15.4 57.4 all-gather.2
  604.9 75.5 reduce-scatter.4
  685.0 76.7 reduce-scatter.2
  766.6 155.0 all-reduce.1
